TPU v7x, 32 devices: a whole 2x2x4 slice. The times are simulated.
32 devices in a mesh: hi: 4 (over y, core), lo: 8 (over z, x).
Axes of the slice: x: 2, y: 2, z: 4, core: 2. Of those that a mesh axis runs over, the one named last changes fastest.
Arguments:
- panel: float32 [262144, 128], P(('hi', 'lo')), may hold values from -6 to 6
- row_signs: float32 [262144, 1], P(('hi', 'lo')), may hold values from -4 to 4
- sample_rows: int32 [1024], replicated, may hold values from 0 to 262143, as said below
Outputs:
- sketch: float32 [1024, 128], P(('hi', 'lo'))
Inputs may be any that keep to these rules, and one draw needn't show every extreme that they name: `sample_rows`: repeats may occur; they fall very unevenly on the devices that hold the rows.
All inputs are finite; a program needn't handle non-finite values.
Results may differ from a plain program's by a relative error of at most 0.000098.
Values sent between devices are 32-bit elements; how exact they have to be, the bound alone decides.
A program may use at most 64 MiB of HBM per device.

v0:
```python
import jax
import jax.numpy as jnp
from jax import lax
from jax.sharding import PartitionSpec as P


def hadamard(order):
    left = jnp.arange(order, dtype=jnp.int32)[:, None]
    right = jnp.arange(order, dtype=jnp.int32)[None, :]
    parity = lax.population_count(left & right) & 1
    return (1 - 2 * parity).astype(jnp.float32)


def local_transform(field):
    count, width = field.shape
    inner = min(count, 128)
    outer = count // inner
    shaped = field.reshape(outer, inner, width)
    step_one = jnp.einsum("eb,abk->aek", hadamard(inner), shaped, precision=lax.Precision.HIGHEST)
    step_two = jnp.einsum("ca,aek->cek", hadamard(outer), step_one, precision=lax.Precision.HIGHEST)
    return step_two.reshape(count, width)


def body(panel, row_signs, sample_rows):
    count, width = panel.shape
    devices = lax.axis_size("hi") * lax.axis_size("lo")
    device_id = lax.axis_index("hi") * lax.axis_size("lo") + lax.axis_index("lo")
    field = local_transform(row_signs * panel)
    rows = jnp.take(field, sample_rows % count, axis=0)
    parity = lax.population_count((sample_rows // count) & device_id) & 1
    sign = (1 - 2 * parity).astype(jnp.float32) / jnp.sqrt(jnp.float32(count * devices))
    return lax.psum_scatter(sign[:, None] * rows, ("hi", "lo"), scatter_dimension=0, tiled=True)


def solution(mesh):
    placed = (P(("hi", "lo"), None), P(("hi", "lo"), None), P())
    return jax.shard_map(
        body, mesh=mesh, in_specs=placed, out_specs=P(("hi", "lo"), None), check_vma=False
    )
```

profile of v0, /device:TPU:0, one launch (start us, length us, event | category | flops | bytes accessed | tf_op | source)
XLA Modules:
  0.0 186.1 jit_solution(18253966997691986031)
XLA Ops:
  6.5 0.0 reduce-scatter.2.cloned.1.call-start
  6.5 0.7 broadcast_clamp_fusion
  7.2 0.7 compare_and_fusion
  7.9 4.7 %broadcast_multiply_fusion = f32[8192,128]{1,0:T(8,128)S(1)} fusion(f32[8192,128]{1,0:T(8,128)} %param.3, f32[8192]{0:T(1024)} %bitcast.15), kind=kLoop, calls=%fused_computation.3 | loop fusion | flops 1048576 | bytes 8421376 | tf_op jit(solution)/shard_map/mul | solution.py:28
  12.6 8.4 %fusion.2 = f32[64,128,128]{2,1,0:T(8,128)} fusion(f32[64,128,128]{2,1,0:T(8,128)S(1)} %bitcast.14), kind=kOutput, calls=%fused_computation.5 | convolution fusion | flops 1610711040 | bytes 8388608 | tf_op jit(solution)/shard_map/eb,abk->aek/dot_general | solution.py:19
  21.0 5.4 %copy.5 = f32[64,128,128]{1,0,2:T(8,128)} copy(f32[64,128,128]{2,1,0:T(8,128)} %fusion.2) | data formatting | bytes 8388608 | tf_op jit(solution)/shard_map/eb,abk->aek/dot_general | solution.py:19
  26.4 5.5 %fusion = f32[64,128,128]{2,0,1:T(8,128)S(1)} fusion(f32[64,128,128]{1,0,2:T(8,128)} %copy.5), kind=kOutput, calls=%fused_computation.1 | convolution fusion | flops 805330944 | bytes 8388608 | tf_op jit(solution)/shard_map/ca,aek->cek/dot_general | solution.py:20
  31.9 0.0 copy-start
  31.9 4.4 %copy.4 = f32[64,128,128]{2,1,0:T(8,128)} copy(f32[64,128,128]{2,0,1:T(8,128)S(1)} %fusion) | data formatting | bytes 8388608 | tf_op jit(solution)/shard_map/ca,aek->cek/dot_general | solution.py:20
  36.2 0.0 copy-done
  36.3 5.0 %gather_fusion = f32[1024,128]{1,0:T(8,128)S(1)} fusion(f32[8192,128]{1,0:T(8,128)} %bitcast.13, s32[1024]{0:T(1024)S(1)} %broadcast_clamp_fusion), kind=kCustom, calls=%fused_computation | custom fusion | bytes 1052672 | tf_op jit(solution)/shard_map/jit(_take)/gather | solution.py:29
  41.3 1.1 select_multiply_fusion
  42.4 0.0 reduce-scatter.2.cloned.1.call-update
  42.4 136.9 %reduce-scatter.2.cloned.1.call-done = f32[32,128]{1,0:T(8,128)} async-done(((f32[1024,128]{1,0:T(8,128)}), f32[32,128]{1,0:T(8,128)}) %reduce-scatter.2.cloned.1.call-update) | async-done | bytes 16400 | tf_op jit(solution)/shard_map/reduce_scatter | solution.py:32
  (1 shorter events, 0.0 us)
Async XLA Ops:
  6.5 172.8 %reduce-scatter.2.cloned.1.call-start = ((), (), s32[]{:S(2)}) async-start(), calls=%async_computation.1 | async-start | bytes 540672 | tf_op jit(solution)/shard_map/reduce_scatter | solution.py:32
  31.9 4.4 %copy-start = (s32[1024]{0:T(1024)S(1)}, s32[1024]{0:T(1024)}, u32[]{:S(2)}) copy-start(s32[1024]{0:T(1024)} %param.5) | copy-start | bytes 12292
Sparse Core Ops, SparseCore 0:
  42.5 136.7 reduce-scatter.1
where the time goes:
time: 186 us
  waiting for transfers between devices  137 us (74%)
  local copies, waits for them, and re-layouts  14.8 us (8%)
  matrix products  13.9 us (7%)
  between operations  13.4 us (7%)
  other arithmetic  7.19 us (4%)
    reduce_scatter x1, waiting for transfers between devices, body(): lax.psum_scatter(sign[:, None] * rows, ('hi', 'lo'), scatter_dimension=0,...  137 us
    dot_general x1, matrix products, local_transform(): jnp.einsum('eb,abk->aek', hadamard(inner), shaped, precision=lax.Precisio...  8.4 us
    dot_general x1, matrix products, local_transform(): jnp.einsum('ca,aek->cek', hadamard(outer), step_one, precision=lax.Precis...  5.46 us
    dot_general x1, local copies, waits for them, and re-layouts, local_transform(): jnp.einsum('eb,abk->aek', hadamard(inner), shaped, precision=lax.Precisio...  5.41 us
    gather x1, local copies, waits for them, and re-layouts, body(): rows = jnp.take(field, sample_rows % count, axis=0)  4.99 us
    mul x1, other arithmetic, body(): field = local_transform(row_signs * panel)  4.65 us
    dot_general x1, local copies, waits for them, and re-layouts, local_transform(): jnp.einsum('ca,aek->cek', hadamard(outer), step_one, precision=lax.Precis...  4.36 us
  transfers between devices with their start and end apart: 1, of which 1 were waited for; matrix products, arithmetic and copies ran while one was open for 0% of the time, Pallas kernels for 0%

commit v1 on v0

v1 whole, which is shorter than its diff:
```python
import functools
import math

import jax
import jax.numpy as jnp
from jax import lax
from jax.experimental import pallas as pl
from jax.experimental.pallas import tpu as pltpu
from jax.sharding import PartitionSpec as P

MESH = pl.DeviceIdType.MESH
LOW = 256
LANES = 128
TILE = 8


def parity_sign(bits):
    shift = 16
    while shift:
        bits = bits ^ (bits >> shift)
        shift //= 2
    return (1 - 2 * (bits & 1)).astype(jnp.float32)


def kernel(hi_count, lo_count, panel_hbm, signs_ref, rows_ref, picks_ref, out_ref,
           panel, field, had, sgn, terms, mine, got_a, got_b, got_c, last,
           load_sem, send_a, recv_a, send_b, recv_b, send_c, recv_c):
    count = panel.shape[0]
    blocks = count // LOW
    share = out_ref.shape[0]
    total = count * hi_count * lo_count
    side = 2 ** ((lo_count.bit_length() - 1) // 2)
    depth = lo_count // side
    plane = (hi_count // 2) * side
    hi, lo = lax.axis_index("hi"), lax.axis_index("lo")
    me = hi * lo_count + lo
    core = hi % 2
    spot = (hi // 2) * side + lo % side
    level = lo // side

    def place(core_to, level_to, spot_to):
        return ((spot_to // side) * 2 + core_to, level_to * side + spot_to % side)

    partner = place(1 - core, level, spot)
    peers_plane = [place(core, level, spot ^ j) for j in range(plane)]
    peers_depth = [place(core, level ^ r, spot) for r in range(depth)]

    loads = len(load_sem_list := [load_sem.at[i] for i in range(load_sem.shape[0])])
    rows_load = count // loads
    copies = []
    for i in range(loads):
        part = pl.ds(i * rows_load, rows_load)
        copy = pltpu.make_async_copy(panel_hbm.at[part], panel.at[part], load_sem_list[i])
        copy.start()
        copies.append(copy)

    barrier = pltpu.get_barrier_semaphore()
    greet = [partner] + peers_plane[1:] + peers_depth[1:]
    for device in greet:
        pl.semaphore_signal(barrier, inc=1, device_id=device, device_id_type=MESH)

    left = lax.broadcasted_iota(jnp.int32, (LOW, LOW), 0)
    right = lax.broadcasted_iota(jnp.int32, (LOW, LOW), 1)
    had[...] = parity_sign(left & right).astype(jnp.bfloat16)

    weight = parity_sign((picks_ref[...] // count) & me) * (1.0 / math.sqrt(total))
    for g in range(weight.shape[0]):
        sgn[pl.ds(g * LANES, LANES), :] = jnp.broadcast_to(weight[g:g + 1, :], (LANES, LANES)).T

    for i in range(loads):
        copies[i].wait()

        @pl.loop(i * (blocks // loads), (i + 1) * (blocks // loads))
        def _(a):
            for h in range(LOW // LANES):
                line = signs_ref[pl.ds(a * (LOW // LANES) + h, 1), :]
                wide = jnp.broadcast_to(line, (LANES, LANES)).T
                part = pl.ds(a * LOW + h * LANES, LANES)
                panel[part, :] = panel[part, :] * wide
            block = panel[pl.ds(a * LOW, LOW), :]
            big = block.astype(jnp.bfloat16)
            small = (block - big.astype(jnp.float32)).astype(jnp.bfloat16)
            both = jnp.concatenate([big, small], axis=1)
            done = jnp.dot(had[...], both, preferred_element_type=jnp.float32)
            field[pl.ds(a * LOW, LOW), :] = done[:, :LANES] + done[:, LANES:]

    @pl.loop(0, LOW // TILE)
    def _(p):
        parts = [field[pl.ds(b * LOW + p * TILE, TILE), :] for b in range(blocks)]
        half = 1
        while half < blocks:
            for b in range(blocks):
                if not b & half:
                    x, y = parts[b], parts[b + half]
                    parts[b], parts[b + half] = x + y, x - y
            half *= 2
        for b in range(blocks):
            field[pl.ds(b * LOW + p * TILE, TILE), :] = parts[b]

    pl.semaphore_wait(barrier, len(greet))

    def gather(dst, core_to, level_to):
        @pl.loop(0, plane)
        def _(j):
            hi_to, lo_to = place(core_to, level_to, spot ^ j)
            start = (hi_to * lo_count + lo_to) * share
            for s in range(share):
                row = rows_ref[start + s] & (count - 1)
                dst[pl.ds(j * share + s, 1), :] = field[pl.ds(row, 1), :]
            part = pl.ds(j * share, share)
            dst[part, :] = dst[part, :] * sgn[pl.ds(start, share), :]

    def remote(src, dst, send, recv, device):
        return pltpu.make_async_remote_copy(
            src_ref=src, dst_ref=dst, send_sem=send, recv_sem=recv,
            device_id=device, device_id_type=MESH)

    order = list(range(1, depth)) + [0]
    sent_b, sent_c = {}, {}

    def finish_plane(r):
        total_rows = mine[r, pl.ds(0, share), :]
        for j in range(1, plane):
            sent_b[r][j].wait_recv()
            total_rows = total_rows + got_b[r, pl.ds(j * share, share), :]
        last[r] = total_rows
        if r:
            sent_c[r] = remote(last.at[r], got_c.at[r], send_c.at[r], recv_c.at[r], peers_depth[r])
            sent_c[r].start()

    sent_a = {}
    previous = None
    for r in order:
        gather(terms.at[r], 1 - core, level ^ r)
        sent_a[r] = remote(terms.at[r], got_a.at[r], send_a.at[r], recv_a.at[r], partner)
        sent_a[r].start()
        gather(mine.at[r], core, level ^ r)
        sent_a[r].wait_recv()
        mine[r] = mine[r] + got_a[r]
        sent_b[r] = {}
        for j in range(1, plane):
            part = pl.ds(j * share, share)
            sent_b[r][j] = remote(mine.at[r, part], got_b.at[r, part],
                                  send_b.at[r, j], recv_b.at[r, j], peers_plane[j])
            sent_b[r][j].start()
        if previous is not None:
            finish_plane(previous)
        previous = r
    finish_plane(previous)
    result = last[0]
    for r in order[:-1]:
        sent_c[r].wait_recv()
        result = result + got_c[r]
    out_ref[...] = result
    for r in order:
        sent_a[r].wait_send()
        for j in range(1, plane):
            sent_b[r][j].wait_send()
        if r:
            sent_c[r].wait_send()


def body(panel, row_signs, sample_rows):
    count, width = panel.shape
    hi_count, lo_count = lax.axis_size("hi"), lax.axis_size("lo")
    kept = sample_rows.shape[0]
    share = kept // (hi_count * lo_count)
    side = 2 ** ((lo_count.bit_length() - 1) // 2)
    depth = lo_count // side
    plane = (hi_count // 2) * side
    loads = 8
    vmem = pl.BlockSpec(memory_space=pltpu.VMEM)
    dma = pltpu.SemaphoreType.DMA
    f32 = jnp.float32
    chunk = (depth, plane * share, width)
    return pl.pallas_call(
        functools.partial(kernel, hi_count, lo_count),
        out_shape=jax.ShapeDtypeStruct((share, width), f32),
        in_specs=[pl.BlockSpec(memory_space=pl.ANY), vmem,
                  pl.BlockSpec(memory_space=pltpu.SMEM), vmem],
        out_specs=vmem,
        scratch_shapes=[
            pltpu.VMEM((count, width), f32),
            pltpu.VMEM((count, width), f32),
            pltpu.VMEM((LOW, LOW), jnp.bfloat16),
            pltpu.VMEM((kept, width), f32),
            pltpu.VMEM(chunk, f32),
            pltpu.VMEM(chunk, f32),
            pltpu.VMEM(chunk, f32),
            pltpu.VMEM(chunk, f32),
            pltpu.VMEM((depth, share, width), f32),
            pltpu.VMEM((depth, share, width), f32),
            dma((loads,)),
            dma((depth,)), dma((depth,)),
            dma((depth, plane)), dma((depth, plane)),
            dma((depth,)), dma((depth,)),
        ],
        compiler_params=pltpu.CompilerParams(
            collective_id=0, has_side_effects=True, vmem_limit_bytes=40 * 2**20),
        cost_estimate=pl.CostEstimate(
            flops=2 * count * LOW * 2 * width, bytes_accessed=count * width * 4, transcendentals=0),
    )(panel, row_signs.reshape(count // LANES, LANES), sample_rows,
      sample_rows.reshape(kept // LANES, LANES))


def solution(mesh):
    placed = (P(("hi", "lo"), None), P(("hi", "lo"), None), P())
    return jax.shard_map(
        body, mesh=mesh, in_specs=placed, out_specs=P(("hi", "lo"), None), check_vma=False
    )
```

time: 186 us -> 32.5 us (0.17)
  waiting for transfers between devices: 137 us -> 0 us
  Pallas kernels: 0 us -> 28 us
  matrix products: 13.9 us -> 0 us
  between operations: 13.4 us -> 0.01 us
  local copies, waits for them, and re-layouts: 14.8 us -> 4.24 us
  other arithmetic: 7.19 us -> 0 us
    reduce_scatter x1 -> x0, waiting for transfers between devices: 137 us -> none  [body(): lax.psum_scatter(sign[:, None] * rows, ('hi', 'lo'), scatter_dimension=0,...]
    pallas_call x0 -> x1, Pallas kernels: none -> 28 us  [body(): pl.pallas_call(functools.partial(kernel, hi_count, lo_count), out_shape=j...]
    dot_general x2 -> x0, matrix products: 13.9 us -> none  [the longest x1 8.4 us: local_transform(): jnp.einsum('eb,abk->aek', hadamard(inner), shaped, precision=lax.Precisio...]
    dot_general x2 -> x0, local copies, waits for them, and re-layouts: 9.77 us -> none  [the longest x1 5.41 us: local_transform(): jnp.einsum('eb,abk->aek', hadamard(inner), shaped, precision=lax.Precisio...]
    mul x2 -> x0, other arithmetic: 5.77 us -> none  [the longest x1 4.65 us: body(): field = local_transform(row_signs * panel)]
    gather x1 -> x0, local copies, waits for them, and re-layouts: 4.99 us -> none  [body(): rows = jnp.take(field, sample_rows % count, axis=0)]
    unnamed x2 -> x7, local copies, waits for them, and re-layouts: 0.01 us -> 4.24 us
  transfers between devices with their start and end apart: 1 -> 0, of which waited for: 1 -> 0; matrix products, arithmetic and copies ran while one was open for 0% -> 0% of each run, Pallas kernels for 0% -> 0%
where the time goes in v1:
time: 32.5 us; the launch traced here: 32.2 us
  Pallas kernels  28 us (86%)
  local copies, waits for them, and re-layouts  4.24 us (13%)
    pallas_call x1, Pallas kernels, body(): pl.pallas_call(functools.partial(kernel, hi_count, lo_count), out_shape=j...  28 us
    unnamed x7, local copies, waits for them, and re-layouts  4.24 us

profile of v1, /device:TPU:0, one launch (start us, length us, event | category | flops | bytes accessed | tf_op | source)
XLA Modules:
  0.0 32.2 jit_solution(5059509868927249535)
XLA Ops:
  0.0 0.0 copy-start
  0.0 2.2 %copy-done = f32[8192,128]{1,0:T(8,128)S(1)} copy-done((f32[8192,128]{1,0:T(8,128)S(1)}, f32[8192,128]{1,0:T(8,128)}, u32[]{:S(2)}) %copy-start) | copy-done | bytes 4194328
  2.2 0.0 copy-start.1
  2.2 0.8 %copy-done.1 = f32[8192,1]{0,1:T(1,128)S(1)} copy-done((f32[8192,1]{0,1:T(1,128)S(1)}, f32[8192,1]{0,1:T(1,128)}, u32[]{:S(2)}) %copy-start.1) | copy-done | bytes 32792
  2.9 0.0 copy-start.2
  2.9 0.7 %copy-done.2 = s32[1024]{0:T(1024)S(1)} copy-done((s32[1024]{0:T(1024)S(1)}, s32[1024]{0:T(1024)}, u32[]{:S(2)}) %copy-start.2) | copy-done | bytes 4120
  3.6 28.0 %shard_map.37 = f32[32,128]{1,0:T(8,128)S(1)} custom-call(f32[8192,128]{1,0:T(8,128)S(1)} %copy-done, f32[64,128]{1,0:T(8,128)S(1)} %bitcast.2, s32[1024]{0:T(1024)S(1)} %copy-done.2, s32[8,128]{1,0:T(8,128)S(1)} %bitcast.3), custom_call_target="tpu_custom_call" | custom-call | flops 1073741824 | bytes 4194304 | tf_op jit(solution)/shard_map/pallas_call | solution.py:176
  31.6 0.6 %copy.5 = f32[32,128]{1,0:T(8,128)} copy(f32[32,128]{1,0:T(8,128)S(1)} %shard_map.37) | data formatting | bytes 32768
Async XLA Ops:
  0.0 2.2 %copy-start = (f32[8192,128]{1,0:T(8,128)S(1)}, f32[8192,128]{1,0:T(8,128)}, u32[]{:S(2)}) copy-start(f32[8192,128]{1,0:T(8,128)} %panel_hbm.1) | copy-start | bytes 12582916
  2.2 0.8 %copy-start.1 = (f32[8192,1]{0,1:T(1,128)S(1)}, f32[8192,1]{0,1:T(1,128)}, u32[]{:S(2)}) copy-start(f32[8192,1]{0,1:T(1,128)} %param.4) | copy-start | bytes 98308
  2.9 0.7 %copy-start.2 = (s32[1024]{0:T(1024)S(1)}, s32[1024]{0:T(1024)}, u32[]{:S(2)}) copy-start(s32[1024]{0:T(1024)} %rows_ref.1) | copy-start | bytes 12292

commit v2 on v1

v2 whole, which is shorter than its diff:
```python
import functools
import math

import jax
import jax.numpy as jnp
from jax import lax
from jax.experimental import pallas as pl
from jax.experimental.pallas import tpu as pltpu
from jax.sharding import PartitionSpec as P

MESH = pl.DeviceIdType.MESH
LOW = 256
LANES = 128
TILE = 8


def parity_sign(bits):
    shift = 16
    while shift:
        bits = bits ^ (bits >> shift)
        shift //= 2
    return (1 - 2 * (bits & 1)).astype(jnp.float32)


def kernel(hi_count, lo_count, panel_hbm, signs_hbm, rows_hbm, picks_hbm, out_ref,
           panel, signs_ref, rows_ref, picks_ref, field, had, sgn, terms, mine, got_a, got_b, got_c, last,
           load_sem, small_sem, send_a, recv_a, send_b, recv_b, send_c, recv_c):
    count = panel.shape[0]
    blocks = count // LOW
    share = out_ref.shape[0]
    total = count * hi_count * lo_count
    side = 2 ** ((lo_count.bit_length() - 1) // 2)
    depth = lo_count // side
    plane = (hi_count // 2) * side
    hi, lo = lax.axis_index("hi"), lax.axis_index("lo")
    me = hi * lo_count + lo
    core = hi % 2
    spot = (hi // 2) * side + lo % side
    level = lo // side

    def place(core_to, level_to, spot_to):
        return ((spot_to // side) * 2 + core_to, level_to * side + spot_to % side)

    partner = place(1 - core, level, spot)
    peers_plane = [place(core, level, spot ^ j) for j in range(plane)]
    peers_depth = [place(core, level ^ r, spot) for r in range(depth)]

    loads = load_sem.shape[0]
    rows_load = count // loads
    small = [pltpu.make_async_copy(signs_hbm, signs_ref, small_sem.at[0]),
             pltpu.make_async_copy(picks_hbm, picks_ref, small_sem.at[1]),
             pltpu.make_async_copy(rows_hbm, rows_ref, small_sem.at[2])]
    for copy in small:
        copy.start()

    def load(i):
        part = pl.ds(i * rows_load, rows_load)
        return pltpu.make_async_copy(panel_hbm.at[part], panel.at[part], load_sem.at[i])

    for i in range(loads):
        load(i).start()

    barrier = pltpu.get_barrier_semaphore()
    greet = [partner] + peers_plane[1:] + peers_depth[1:]
    for device in greet:
        pl.semaphore_signal(barrier, inc=1, device_id=device, device_id_type=MESH)

    left = lax.broadcasted_iota(jnp.int32, (LOW, LOW), 0)
    right = lax.broadcasted_iota(jnp.int32, (LOW, LOW), 1)
    had[...] = parity_sign(left & right).astype(jnp.bfloat16)

    for copy in small:
        copy.wait()

    weight = parity_sign((picks_ref[...] // count) & me) * (1.0 / math.sqrt(total))
    for g in range(weight.shape[0]):
        sgn[pl.ds(g * LANES, LANES), :] = jnp.broadcast_to(weight[g:g + 1, :], (LANES, LANES)).T

    @pl.loop(0, loads)
    def _(i):
        load(i).wait()
        for step in range(blocks // loads):
            a = i * (blocks // loads) + step
            parts = []
            for h in range(LOW // LANES):
                line = signs_ref[pl.ds(a * (LOW // LANES) + h, 1), :]
                wide = jnp.broadcast_to(line, (LANES, LANES)).T
                parts.append(panel[pl.ds(a * LOW + h * LANES, LANES), :] * wide)
            block = jnp.concatenate(parts, axis=0)
            big = block.astype(jnp.bfloat16)
            small = (block - big.astype(jnp.float32)).astype(jnp.bfloat16)
            both = jnp.concatenate([big, small], axis=1)
            done = jnp.dot(had[...], both, preferred_element_type=jnp.float32)
            field[pl.ds(a * LOW, LOW), :] = done[:, :LANES] + done[:, LANES:]

    @pl.loop(0, LOW // TILE)
    def _(p):
        parts = [field[pl.ds(b * LOW + p * TILE, TILE), :] for b in range(blocks)]
        half = 1
        while half < blocks:
            for b in range(blocks):
                if not b & half:
                    x, y = parts[b], parts[b + half]
                    parts[b], parts[b + half] = x + y, x - y
            half *= 2
        for b in range(blocks):
            field[pl.ds(b * LOW + p * TILE, TILE), :] = parts[b]

    pl.semaphore_wait(barrier, len(greet))

    def gather(dst, core_to, level_to):
        @pl.loop(0, plane)
        def _(j):
            hi_to, lo_to = place(core_to, level_to, spot ^ j)
            start = (hi_to * lo_count + lo_to) * share
            for s in range(share):
                row = rows_ref[start + s] & (count - 1)
                dst[pl.ds(j * share + s, 1), :] = field[pl.ds(row, 1), :]
            part = pl.ds(j * share, share)
            dst[part, :] = dst[part, :] * sgn[pl.ds(start, share), :]

    def remote(src, dst, send, recv, device):
        return pltpu.make_async_remote_copy(
            src_ref=src, dst_ref=dst, send_sem=send, recv_sem=recv,
            device_id=device, device_id_type=MESH)

    levels = range(depth)
    sent_a, sent_b = {}, {}

    def send_pair(c):
        gather(terms.at[c], 1 - core, c)
        sent_a[c] = remote(terms.at[c], got_a.at[c], send_a.at[c], recv_a.at[c], partner)
        sent_a[c].start()
        gather(mine.at[c], core, c)

    def send_plane(c):
        sent_a[c].wait_recv()
        for j in list(range(1, plane)) + [0]:
            part = pl.ds(j * share, share)
            mine[c, part, :] = mine[c, part, :] + got_a[c, part, :]
            if j:
                sent_b[c, j] = remote(mine.at[c, part], got_b.at[c, part],
                                      send_b.at[c, j], recv_b.at[c, j], peers_plane[j])
                sent_b[c, j].start()

    def to_level(c):
        return remote(last.at[c], got_c.at[level], send_c.at[c], recv_c.at[level],
                      place(core, c, spot))

    def send_level(c):
        rows = mine[c, pl.ds(0, share), :]
        for j in range(1, plane):
            sent_b[c, j].wait_recv()
            rows = rows + got_b[c, pl.ds(j * share, share), :]
        last[c] = rows

        @pl.when(level != c)
        def _():
            to_level(c).start()

    for c in levels:
        send_pair(c)
        if c:
            send_plane(c - 1)
    send_plane(depth - 1)
    for c in levels:
        send_level(c)
    result = last[level]
    for r in range(1, depth):
        other = level ^ r
        remote(last.at[other], got_c.at[other], send_c.at[other], recv_c.at[other],
               place(core, other, spot)).wait_recv()
        result = result + got_c[other]
    out_ref[...] = result
    for c in levels:
        sent_a[c].wait_send()
        for j in range(1, plane):
            sent_b[c, j].wait_send()

        @pl.when(level != c)
        def _():
            to_level(c).wait_send()


def body(panel, row_signs, sample_rows):
    count, width = panel.shape
    hi_count, lo_count = lax.axis_size("hi"), lax.axis_size("lo")
    kept = sample_rows.shape[0]
    share = kept // (hi_count * lo_count)
    side = 2 ** ((lo_count.bit_length() - 1) // 2)
    depth = lo_count // side
    plane = (hi_count // 2) * side
    loads = 2
    vmem = pl.BlockSpec(memory_space=pltpu.VMEM)
    dma = pltpu.SemaphoreType.DMA
    f32 = jnp.float32
    chunk = (depth, plane * share, width)
    return pl.pallas_call(
        functools.partial(kernel, hi_count, lo_count),
        out_shape=jax.ShapeDtypeStruct((share, width), f32),
        in_specs=[pl.BlockSpec(memory_space=pltpu.HBM)] * 4,
        out_specs=vmem,
        scratch_shapes=[
            pltpu.VMEM((count, width), f32),
            pltpu.VMEM((count // LANES, LANES), f32),
            pltpu.SMEM((kept,), jnp.int32),
            pltpu.VMEM((kept // LANES, LANES), jnp.int32),
            pltpu.VMEM((count, width), f32),
            pltpu.VMEM((LOW, LOW), jnp.bfloat16),
            pltpu.VMEM((kept, width), f32),
            pltpu.VMEM(chunk, f32),
            pltpu.VMEM(chunk, f32),
            pltpu.VMEM(chunk, f32),
            pltpu.VMEM(chunk, f32),
            pltpu.VMEM((depth, share, width), f32),
            pltpu.VMEM((depth, share, width), f32),
            dma((loads,)), dma((3,)),
            dma((depth,)), dma((depth,)),
            dma((depth, plane)), dma((depth, plane)),
            dma((depth,)), dma((depth,)),
        ],
        compiler_params=pltpu.CompilerParams(
            collective_id=0, has_side_effects=True, vmem_limit_bytes=60 * 2**20),
        cost_estimate=pl.CostEstimate(
            flops=2 * count * LOW * 2 * width, bytes_accessed=count * width * 4, transcendentals=0),
    )(panel, row_signs.reshape(count // LANES, LANES), sample_rows,
      sample_rows.reshape(kept // LANES, LANES))


def solution(mesh):
    placed = (P(("hi", "lo"), None), P(("hi", "lo"), None), P())
    return jax.shard_map(
        body, mesh=mesh, in_specs=placed, out_specs=P(("hi", "lo"), None), check_vma=False
    )
```

time: 32.5 us -> 19.8 us (0.61)
  Pallas kernels: 28 us -> 18.2 us
  local copies, waits for them, and re-layouts: 4.24 us -> 1.32 us
    pallas_call x1, Pallas kernels: 28 us -> 18.2 us  [body(): pl.pallas_call(functools.partial(kernel, hi_count, lo_count), out_shape=j...]
    unnamed x7 -> x1, local copies, waits for them, and re-layouts: 4.24 us -> 1.32 us
where the time goes in v2:
time: 19.8 us; the launch traced here: 19.5 us
  Pallas kernels  18.2 us (92%)
  local copies, waits for them, and re-layouts  1.32 us (7%)
    pallas_call x1, Pallas kernels, body(): pl.pallas_call(functools.partial(kernel, hi_count, lo_count), out_shape=j...  18.2 us
    unnamed x1, local copies, waits for them, and re-layouts  1.32 us

profile of v2, /device:TPU:0, one launch (start us, length us, event | category | flops | bytes accessed | tf_op | source)
XLA Modules:
  0.0 19.5 jit_solution(10449613144192612272)
XLA Ops:
  0.0 18.2 %shard_map.37 = f32[32,128]{1,0:T(8,128)} custom-call(f32[8192,128]{1,0:T(8,128)} %panel_hbm.1, f32[64,128]{1,0:T(8,128)} %bitcast.2, s32[1024]{0:T(1024)} %rows_hbm.1, s32[8,128]{1,0:T(8,128)} %bitcast.3), custom_call_target="tpu_custom_call" | custom-call | flops 1073741824 | bytes 4194304 | tf_op jit(solution)/shard_map/pallas_call | solution.py:198
  18.2 1.3 %copy.5 = f32[32,128]{1,0:T(8,128)} copy(f32[32,128]{1,0:T(8,128)} %shard_map.37) | data formatting | bytes 32768

commit v3 on v2

--- a/solution.py
+++ b/solution.py
@@ -131,6 +131,8 @@
         gather(terms.at[c], 1 - core, c)
         sent_a[c] = remote(terms.at[c], got_a.at[c], send_a.at[c], recv_a.at[c], partner)
         sent_a[c].start()
+        if c:
+            send_plane(c - 1)
         gather(mine.at[c], core, c)
 
     def send_plane(c):
@@ -160,8 +162,6 @@
 
     for c in levels:
         send_pair(c)
-        if c:
-            send_plane(c - 1)
     send_plane(depth - 1)
     for c in levels:
         send_level(c)

time: 19.8 us -> 19.6 us (0.990)
  Pallas kernels: 18.2 us -> 18 us
    pallas_call x1, Pallas kernels: 18.2 us -> 18 us  [body(): pl.pallas_call(functools.partial(kernel, hi_count, lo_count), out_shape=j...]
where the time goes in v3:
time: 19.6 us; the launch traced here: 19.3 us
  Pallas kernels  18 us (92%)
  local copies, waits for them, and re-layouts  1.32 us (7%)
    pallas_call x1, Pallas kernels, body(): pl.pallas_call(functools.partial(kernel, hi_count, lo_count), out_shape=j...  18 us
    unnamed x1, local copies, waits for them, and re-layouts  1.32 us

profile of v3, /device:TPU:0, one launch (start us, length us, event | category | flops | bytes accessed | tf_op | source)
XLA Modules:
  0.0 19.3 jit_solution(12939989003301019752)
XLA Ops:
  0.0 18.0 %shard_map.37 = f32[32,128]{1,0:T(8,128)} custom-call(f32[8192,128]{1,0:T(8,128)} %panel_hbm.1, f32[64,128]{1,0:T(8,128)} %bitcast.2, s32[1024]{0:T(1024)} %rows_hbm.1, s32[8,128]{1,0:T(8,128)} %bitcast.3), custom_call_target="tpu_custom_call" | custom-call | flops 1073741824 | bytes 4194304 | tf_op jit(solution)/shard_map/pallas_call | solution.py:198
  18.0 1.3 %copy.5 = f32[32,128]{1,0:T(8,128)} copy(f32[32,128]{1,0:T(8,128)} %shard_map.37) | data formatting | bytes 32768
